TPU v7x, 512 devices: a whole 4x8x8 slice. The times are simulated.
512 devices in a mesh: ctx: 32 (over y, x), dp: 16 (over z, core).
Axes of the slice: x: 4, y: 8, z: 8, core: 2. Of those that a mesh axis runs over, the one named last changes fastest.
Arguments:
- queries: bfloat16 [32, 16, 2304, 128], P('dp', None, 'ctx'), may hold values from -6 to 6
- keys: bfloat16 [32, 16, 2304, 128], P('dp', None, 'ctx'), may hold values from -6 to 6
- values: bfloat16 [32, 16, 2304, 128], P('dp', None, 'ctx'), may hold values from -6 to 6
- out_grad: bfloat16 [32, 16, 2304, 128], P('dp', None, 'ctx'), may hold values from -6 to 6
- gains: float32 [2, 128], replicated, may hold values from 0.5 to 8, as said below
- keep_order: int32 [32, 32, 72], P('dp'), may hold values from 0 to 71, each once within a row
- keep_count: int32 [32, 32], P('dp'), may hold values from 1 to 54, 1152 in all within a row
Outputs:
- attn_out: bfloat16 [32, 16, 2304, 128], P('dp', None, 'ctx')
- query_grad: bfloat16 [32, 16, 2304, 128], P('dp', None, 'ctx')
- key_grad: bfloat16 [32, 16, 2304, 128], P('dp', None, 'ctx')
- value_grad: bfloat16 [32, 16, 2304, 128], P('dp', None, 'ctx')
- gain_grad: float32 [2, 128], replicated
Inputs may be any that keep to these rules, and one draw needn't show every extreme that they name: `keep_order`: each row lists the 72 positions of one shard once; its first keep_count entries are that shard's kept tokens, in rank order. `keep_count`: for each sample the counts sum to 1152; some shard of every sample holds exactly 54. `gains`: Positive.
All inputs are finite; a program needn't handle non-finite values.
Results may differ from a plain program's by a relative error of at most 0.017.
The roundings to bfloat16 on the way count: a program that leaves them out, or rounds other values in their place, can miss the bound.
Values may be sent and summed in bfloat16 or wider, within the bound.
A program may use at most 64 MiB of HBM per device.

v0:
```python
import math

import jax
import jax.numpy as jnp
from jax import lax
from jax.sharding import PartitionSpec as P

EPS = 1e-06


def dot_last(left, right):
    return lax.dot_general(
        left, right, (((1,), (1,)), ((), ())), preferred_element_type=jnp.float32
    )


def dot_first(left, right):
    return lax.dot_general(
        left, right, (((0,), (0,)), ((), ())), preferred_element_type=jnp.float32
    )


def normalize(rows, gain):
    upcast = rows.astype(jnp.float32)
    inv_rms = lax.rsqrt(jnp.mean(upcast * upcast, axis=-1, keepdims=True) + EPS)
    unit = upcast * inv_rms
    return ((unit * gain).astype(jnp.bfloat16), unit, inv_rms)


def norm_back(grad_norm, unit, inv_rms, gain):
    tangent = grad_norm * gain
    return (inv_rms * (tangent - unit * jnp.mean(tangent * unit, axis=-1, keepdims=True))).astype(
        jnp.bfloat16
    )


def block_size(kept_rows):
    return math.gcd(kept_rows, 512)


def softmax_rows(query_block, key_norm, scale):
    scores = dot_last(query_block, key_norm) * scale
    peak = jnp.max(scores, axis=-1, keepdims=True)
    expo = jnp.exp(scores - peak)
    total = jnp.sum(expo, axis=-1, keepdims=True)
    return (expo / total, peak, total)


def back_block(prob, query_block, grad_block, key_norm, value_rows, scale):
    weights = prob.astype(jnp.bfloat16)
    value_part = dot_first(weights, grad_block)
    dprob = dot_last(grad_block, value_rows)
    delta = jnp.sum(prob * dprob, axis=-1, keepdims=True)
    dscore = (prob * (dprob - delta)).astype(jnp.bfloat16)
    query_part = jnp.dot(dscore, key_norm, preferred_element_type=jnp.float32) * scale
    key_part = dot_first(dscore, query_block)
    return (value_part, query_part, key_part)


def finish(grad_qn, grad_kn, value_acc, unit_q, inv_q, unit_k, inv_k, gains):
    gain_part = jnp.stack([jnp.sum(grad_qn * unit_q, axis=0), jnp.sum(grad_kn * unit_k, axis=0)])
    query_grad = norm_back(grad_qn, unit_q, inv_q, gains[0])
    key_grad = norm_back(grad_kn, unit_k, inv_k, gains[1])
    return (query_grad, key_grad, value_acc.astype(jnp.bfloat16), gain_part)


def joined(rows, gains):
    query_rows, key_rows, value_rows, grad_rows = rows
    kept_rows, head_dim = query_rows.shape
    scale = head_dim ** (-0.5)
    block = block_size(kept_rows)
    query_norm, unit_q, inv_q = normalize(query_rows, gains[0])
    key_norm, unit_k, inv_k = normalize(key_rows, gains[1])

    def step(carry, index):
        start = index * block
        query_block = lax.dynamic_slice_in_dim(query_norm, start, block, 0)
        grad_block = lax.dynamic_slice_in_dim(grad_rows, start, block, 0)
        prob, peak, total = softmax_rows(query_block, key_norm, scale)
        out_block = jnp.dot(
            prob.astype(jnp.bfloat16), value_rows, preferred_element_type=jnp.float32
        ).astype(jnp.bfloat16)
        value_part, query_part, key_part = back_block(
            prob, query_block, grad_block, key_norm, value_rows, scale
        )
        return ((carry[0] + key_part, carry[1] + value_part), (out_block, query_part))

    empty = jnp.zeros((kept_rows, head_dim), jnp.float32)
    carry, stacked = lax.scan(step, (empty, empty), jnp.arange(kept_rows // block))
    attended = stacked[0].reshape(kept_rows, head_dim)
    grad_qn = stacked[1].reshape(kept_rows, head_dim)
    rest = finish(grad_qn, carry[0] * scale, carry[1], unit_q, inv_q, unit_k, inv_k, gains)
    return (attended,) + rest


def body(queries, keys, values, out_grad, gains, keep_order, keep_count):
    devices = lax.axis_size("ctx")
    own_index = lax.axis_index("ctx")
    samples, head_count, shard_len, head_dim = queries.shape
    pair_count = samples * head_count
    own_pairs = pair_count // devices
    kept_rows = devices * shard_len // 2
    ending = jnp.cumsum(keep_count, axis=1)
    starting = ending - keep_count
    ranks = jnp.arange(kept_rows, dtype=jnp.int32)
    source = jnp.sum((ending[:, None, :] <= ranks[None, :, None]).astype(jnp.int32), axis=2)
    within = ranks[None, :] - jnp.take_along_axis(starting, source, axis=1)
    slot_of = jnp.argsort(keep_order, axis=-1)
    pair_sample = (own_index * own_pairs + jnp.arange(own_pairs, dtype=jnp.int32)) // head_count
    picked = jnp.take_along_axis(
        keep_order.reshape(samples, devices * shard_len), source * shard_len + within, axis=1
    )
    rows_all = source * shard_len + picked
    arrived = (
        lax.all_to_all(
            queries.reshape(pair_count, shard_len, head_dim),
            "ctx",
            split_axis=0,
            concat_axis=1,
            tiled=True,
        ),
        lax.all_to_all(
            keys.reshape(pair_count, shard_len, head_dim),
            "ctx",
            split_axis=0,
            concat_axis=1,
            tiled=True,
        ),
        lax.all_to_all(
            values.reshape(pair_count, shard_len, head_dim),
            "ctx",
            split_axis=0,
            concat_axis=1,
            tiled=True,
        ),
        lax.all_to_all(
            out_grad.reshape(pair_count, shard_len, head_dim),
            "ctx",
            split_axis=0,
            concat_axis=1,
            tiled=True,
        ),
    )
    home_live = slot_of < keep_count[:, :, None]
    home_rank = starting[:, :, None] + slot_of
    rows_mine = rows_all[pair_sample]
    compact = tuple(
        (jnp.take_along_axis(piece, rows_mine[:, :, None], axis=1) for piece in arrived)
    )
    home_index = jnp.minimum(home_rank, kept_rows - 1).reshape(samples, devices * shard_len)[
        pair_sample
    ]
    home_mask = home_live.reshape(samples, devices * shard_len)[pair_sample]

    def spread(result):
        taken = jnp.take_along_axis(result, home_index[:, :, None], axis=1)
        return jnp.where(home_mask[:, :, None], taken, jnp.zeros((), jnp.bfloat16))

    attended, query_grad, key_grad, value_grad, gain_part = lax.map(
        lambda item: joined(item, gains), compact
    )
    returned = (
        lax.all_to_all(spread(attended), "ctx", split_axis=1, concat_axis=0, tiled=True),
        lax.all_to_all(spread(query_grad), "ctx", split_axis=1, concat_axis=0, tiled=True),
        lax.all_to_all(spread(key_grad), "ctx", split_axis=1, concat_axis=0, tiled=True),
        lax.all_to_all(spread(value_grad), "ctx", split_axis=1, concat_axis=0, tiled=True),
    )
    gain_grad = lax.psum(jnp.sum(gain_part, axis=0), ("ctx", "dp"))
    outputs = tuple((piece.reshape(samples, head_count, shard_len, head_dim) for piece in returned))
    return (outputs[0], outputs[1], outputs[2], outputs[3], gain_grad)


def solution(mesh):
    placed = (
        P("dp", None, "ctx", None),
        P("dp", None, "ctx", None),
        P("dp", None, "ctx", None),
        P("dp", None, "ctx", None),
        P(),
        P("dp", None, None),
        P("dp", None),
    )
    return jax.shard_map(
        body,
        mesh=mesh,
        in_specs=placed,
        out_specs=(
            P("dp", None, "ctx", None),
            P("dp", None, "ctx", None),
            P("dp", None, "ctx", None),
            P("dp", None, "ctx", None),
            P(),
        ),
        check_vma=False,
    )
```

profile of v0, /device:TPU:1, one launch (start us, length us, event | category | flops | bytes accessed | tf_op | source)
XLA Modules:
  0.0 468.1 jit_solution(8666828131007276712)
XLA Ops:
  0.6 28.0 %all_to_all.84 = bf16[32,72,128]{2,1,0:T(8,128)(2,1)S(1)} all-to-all(bf16[32,72,128]{2,1,0:T(8,128)(2,1)} %bitcast.210), channel_id=1, replica_groups=mesh['ctx'=32,'dp'=16] {'ctx'}, dimensions={0} | all-to-all | bytes 1179648 | tf_op jit(solution)/shard_map/all_to_all | solution.py:115
  28.6 5.4 %all-to-all-start.2 = ((bf16[32,72,128]{2,1,0:T(8,128)(2,1)}), bf16[32,72,128]{2,1,0:T(8,128)(2,1)S(1)}, u32[]{:S(2)}, u32[]{:S(2)}) async-start(bf16[32,72,128]{2,1,0:T(8,128)(2,1)} %bitcast.18), calls=%async_computation.2 | async-start | bytes 1179648 | tf_op jit(solution)/shard_map/all_to_all | solution.py:136
  34.5 16.1 %all-to-all-done.2 = bf16[32,72,128]{2,1,0:T(8,128)(2,1)S(1)} async-done(((bf16[32,72,128]{2,1,0:T(8,128)(2,1)}), bf16[32,72,128]{2,1,0:T(8,128)(2,1)S(1)}, u32[]{:S(2)}, u32[]{:S(2)}) %all-to-all-start.2) | async-done | bytes 589856 | tf_op jit(solution)/shard_map/all_to_all | solution.py:136
  50.6 6.3 %all-to-all-start.3 = ((bf16[32,72,128]{2,1,0:T(8,128)(2,1)}), bf16[32,72,128]{2,1,0:T(8,128)(2,1)S(1)}, u32[]{:S(2)}, u32[]{:S(2)}) async-start(bf16[32,72,128]{2,1,0:T(8,128)(2,1)} %bitcast.23), calls=%async_computation.3 | async-start | bytes 1179648 | tf_op jit(solution)/shard_map/all_to_all | solution.py:129
  57.0 18.8 %gather_fusion = s32[2304]{0:T(1024)S(1)} fusion(s32[2,32]{1,0:T(2,128)S(1)} %sub.55, s32[2304]{0:T(1024)S(1)} %reshape.528), kind=kCustom, calls=%fused_computation.8 | custom fusion | bytes 36864 | tf_op jit(solution)/shard_map/jit(take_along_axis)/gather | solution.py:107
  76.0 19.0 %gather_fusion.1 = s32[2304]{0:T(1024)S(1)} fusion(s32[2,2304]{1,0:T(2,128)S(1)} %reshape.371, s32[2304]{0:T(1024)S(1)} %reshape.534), kind=kCustom, calls=%fused_computation.9 | custom fusion | bytes 36864 | tf_op jit(solution)/shard_map/jit(take_along_axis)/gather | solution.py:110
  95.0 9.5 %all-to-all-start.1 = ((bf16[32,72,128]{2,1,0:T(8,128)(2,1)}), bf16[32,72,128]{2,1,0:T(8,128)(2,1)}, u32[]{:S(2)}, u32[]{:S(2)}) async-start(bf16[32,72,128]{2,1,0:T(8,128)(2,1)} %bitcast.11), calls=%async_computation.1 | async-start | bytes 1179648 | tf_op jit(solution)/shard_map/all_to_all | solution.py:122
  110.1 2.9 gather_fusion.2
  113.1 2.9 gather_fusion.4
  116.0 3.4 gather_fusion.5
  120.0 3.7 gather_fusion.3
  126.9 63.3 %while.34 = (s32[]{:T(128)}, f32[1152,128]{1,0:T(8,128)S(1)}, f32[1152,128]{1,0:T(8,128)}, bf16[9,128,128]{2,1,0:T(8,128)(2,1)S(1)}, f32[9,128,128]{2,1,0:T(8,12...) while((s32[]{:T(128)}, f32[1152,128]{1,0:T(8,128)S(1)}, ...), condition=%wide.region_9.11_spmd.clone, body=%wide.region_5.10_spmd.clone.sunk | while | flops 229916288 | bytes 10560626 | solution.py:89
  193.9 4.7 gather_fusion.8
  199.6 4.7 gather_fusion.7
  204.4 4.7 gather_fusion.9
  209.1 4.7 gather_fusion.6
  213.8 2.8 fusion.30
  216.5 9.4 %copy.48 = bf16[1,2304,128]{2,0,1:T(2,128)(2,1)S(1)} copy(bf16[1,2304,128]{2,1,0:T(8,128)(2,1)S(1)} %get-tuple-element.206) | data formatting | bytes 1179648 | tf_op jit(solution)/shard_map/jit(_where)/select_n | solution.py:157
  226.4 13.1 %reduce.11 = bf16[2304,128]{1,0:T(8,128)(2,1)S(1)} reduce(bf16[2304,1,128]{2,1,0:T(2,128)(2,1)S(1)} %bitcast.196, bf16[]{:T(256)} %broadcast.439), dimensions={1}, to_apply=%bitcast.172.reduce_sub_computation | reduce | bytes 1179650
  240.5 8.4 %all-to-all-start.4 = ((bf16[32,2,4608]{2,1,0:T(2,128)(2,1)}), bf16[32,2,4608]{2,1,0:T(2,128)(2,1)S(1)}, u32[]{:S(2)}, u32[]{:S(2)}) async-start(bf16[32,2,4608]{2,1,0:T(2,128)(2,1)} %reshape.594), calls=%async_computation.4 | async-start | bytes 1179648 | tf_op jit(solution)/shard_map/all_to_all | solution.py:163
  249.0 9.5 %copy.47 = bf16[1,2304,128]{2,0,1:T(2,128)(2,1)S(1)} copy(bf16[1,2304,128]{2,1,0:T(8,128)(2,1)S(1)} %copy-done.3) | data formatting | bytes 1179648 | tf_op jit(solution)/shard_map/jit(_where)/select_n | solution.py:157
  258.5 13.7 %reduce.12 = bf16[2304,128]{1,0:T(8,128)(2,1)} reduce(bf16[2304,1,128]{2,1,0:T(2,128)(2,1)S(1)} %bitcast.198, bf16[]{:T(256)} %broadcast.439), dimensions={1}, to_apply=%bitcast.171.reduce_sub_computation | reduce | bytes 1179650
  272.2 2.6 reshape.596
  274.7 9.6 %all-to-all-start.5 = ((bf16[32,2,4608]{2,1,0:T(2,128)(2,1)}), bf16[32,2,4608]{2,1,0:T(2,128)(2,1)}, u32[]{:S(2)}, u32[]{:S(2)}) async-start(bf16[32,2,4608]{2,1,0:T(2,128)(2,1)} %reshape.596), calls=%async_computation.5 | async-start | bytes 1179648 | tf_op jit(solution)/shard_map/all_to_all | solution.py:164
  284.3 9.5 %copy.46 = bf16[1,2304,128]{2,0,1:T(2,128)(2,1)S(1)} copy(bf16[1,2304,128]{2,1,0:T(8,128)(2,1)S(1)} %copy-done.2) | data formatting | bytes 1179648 | tf_op jit(solution)/shard_map/jit(_where)/select_n | solution.py:157
  293.8 12.9 %reduce.13 = bf16[2304,128]{1,0:T(8,128)(2,1)S(1)} reduce(bf16[2304,1,128]{2,1,0:T(2,128)(2,1)S(1)} %bitcast.199, bf16[]{:T(256)} %broadcast.439), dimensions={1}, to_apply=%bitcast.170.reduce_sub_computation | reduce | bytes 1179650
  307.7 8.9 %all-to-all-start.6 = ((bf16[32,2,4608]{2,1,0:T(2,128)(2,1)}), bf16[32,2,4608]{2,1,0:T(2,128)(2,1)S(1)}, u32[]{:S(2)}, u32[]{:S(2)}) async-start(bf16[32,2,4608]{2,1,0:T(2,128)(2,1)} %reshape.598), calls=%async_computation.6 | async-start | bytes 1179648 | tf_op jit(solution)/shard_map/all_to_all | solution.py:165
  316.6 9.5 %copy.45 = bf16[1,2304,128]{2,0,1:T(2,128)(2,1)S(1)} copy(bf16[1,2304,128]{2,1,0:T(8,128)(2,1)S(1)} %get-tuple-element.203) | data formatting | bytes 1179648 | tf_op jit(solution)/shard_map/jit(_where)/select_n | solution.py:157
  326.0 12.9 %reduce.14 = bf16[2304,128]{1,0:T(8,128)(2,1)S(1)} reduce(bf16[2304,1,128]{2,1,0:T(2,128)(2,1)S(1)} %bitcast.197, bf16[]{:T(256)} %broadcast.439), dimensions={1}, to_apply=%bitcast.169.reduce_sub_computation | reduce | bytes 1179650
  339.9 9.2 %all-to-all-start.7 = ((bf16[32,2,4608]{2,1,0:T(2,128)(2,1)}), bf16[32,2,4608]{2,1,0:T(2,128)(2,1)S(1)}, u32[]{:S(2)}, u32[]{:S(2)}) async-start(bf16[32,2,4608]{2,1,0:T(2,128)(2,1)} %reshape.600), calls=%async_computation.7 | async-start | bytes 1179648 | tf_op jit(solution)/shard_map/all_to_all | solution.py:166
  349.1 110.1 %psum.7 = f32[2,128]{1,0:T(2,128)} all-reduce(f32[2,128]{1,0:T(2,128)S(1)} %pad_maximum_fusion), channel_id=1, replica_groups=mesh['ctx'=32,'dp'=16] {'ctx','dp'}, use_global_device_ids=true, to_apply=%region_14.17 | all-reduce | flops 256 | bytes 2048 | tf_op jit(solution)/shard_map/psum | solution.py:168
  460.6 3.8 reshape.597
  (261 shorter events, 79.6 us)
Async XLA Ops:
  0.6 33.5 %copy-start.19 = (s32[2,32]{1,0:T(2,128)S(1)}, s32[2,32]{1,0:T(2,128)}, u32[]{:S(2)}) copy-start(s32[2,32]{1,0:T(2,128)} %param.19) | copy-start | bytes 772
  28.6 21.9 %all-to-all-start.2 = ((bf16[32,72,128]{2,1,0:T(8,128)(2,1)}), bf16[32,72,128]{2,1,0:T(8,128)(2,1)S(1)}, u32[]{:S(2)}, u32[]{:S(2)}) async-start(bf16[32,72,128]{2,1,0:T(8,128)(2,1)} %bitcast.18), calls=%async_computation.2 | async-start | bytes 1179648 | tf_op jit(solution)/shard_map/all_to_all | solution.py:136
  50.6 44.4 %all-to-all-start.3 = ((bf16[32,72,128]{2,1,0:T(8,128)(2,1)}), bf16[32,72,128]{2,1,0:T(8,128)(2,1)S(1)}, u32[]{:S(2)}, u32[]{:S(2)}) async-start(bf16[32,72,128]{2,1,0:T(8,128)(2,1)} %bitcast.23), calls=%async_computation.3 | async-start | bytes 1179648 | tf_op jit(solution)/shard_map/all_to_all | solution.py:129
  56.9 18.9 %copy-start.10 = (s32[2,32,72]{2,1,0:T(8,128)S(1)}, s32[2,32,72]{2,1,0:T(8,128)}, u32[]{:S(2)}) copy-start(s32[2,32,72]{2,1,0:T(8,128)} %param.18) | copy-start | bytes 55300
  94.9 14.0 %copy-start.23 = (f32[2,128]{1,0:T(2,128)S(1)}, f32[2,128]{1,0:T(2,128)}, u32[]{:S(2)}) copy-start(f32[2,128]{1,0:T(2,128)} %param.17) | copy-start | bytes 3076
  95.0 25.0 %all-to-all-start.1 = ((bf16[32,72,128]{2,1,0:T(8,128)(2,1)}), bf16[32,72,128]{2,1,0:T(8,128)(2,1)}, u32[]{:S(2)}, u32[]{:S(2)}) async-start(bf16[32,72,128]{2,1,0:T(8,128)(2,1)} %bitcast.11), calls=%async_computation.1 | async-start | bytes 1179648 | tf_op jit(solution)/shard_map/all_to_all | solution.py:122
  104.6 21.3 %copy-start.11 = (pred[1152]{0:T(1024)(128)(4,1)}, pred[1152]{0:T(1024)(128)(4,1)S(1)}, u32[]{:S(2)}) copy-start(pred[1152]{0:T(1024)(128)(4,1)S(1)} %get-tuple-element.193) | copy-start | bytes 3460
  108.9 4.1 copy-start.7
  113.0 12.8 %copy-start = (bf16[1152,128]{1,0:T(8,128)(2,1)}, bf16[1152,128]{1,0:T(8,128)(2,1)S(1)}, u32[]{:S(2)}) copy-start(bf16[1152,128]{1,0:T(8,128)(2,1)S(1)} %gather_fusion.2) | copy-start | bytes 884740
  116.0 4.0 copy-start.8
  124.2 2.7 copy-start.4
  143.1 2.3 copy-start.15
  150.1 2.3 copy-start.15
  157.2 2.3 copy-start.15
  164.3 2.3 copy-start.15
  171.3 2.3 copy-start.15
  178.4 2.3 copy-start.15
  185.5 2.3 copy-start.15
  190.2 3.3 copy-start.16
  190.2 3.3 copy-start.21
  193.9 4.7 %copy-start.1 = (bf16[1152,128]{1,0:T(8,128)(2,1)S(1)}, bf16[1152,128]{1,0:T(8,128)(2,1)}, u32[]{:S(2)}) copy-start(bf16[1152,128]{1,0:T(8,128)(2,1)} %copy-done) | copy-start | bytes 884740
  193.9 4.7 %copy-start.12 = (pred[1152]{0:T(1024)(128)(4,1)S(1)}, pred[1152]{0:T(1024)(128)(4,1)}, u32[]{:S(2)}) copy-start(pred[1152]{0:T(1024)(128)(4,1)} %copy-done.11) | copy-start | bytes 3460
  193.9 4.7 %copy-start.14 = (f32[1152]{0:T(1024)S(1)}, f32[1152]{0:T(1024)}, u32[]{:S(2)}) copy-start(f32[1152]{0:T(1024)} %copy-done.13) | copy-start | bytes 13828
  199.6 4.7 %copy-start.5 = (f32[1152,128]{1,0:T(8,128)S(1)}, f32[1152,128]{1,0:T(8,128)}, u32[]{:S(2)}) copy-start(f32[1152,128]{1,0:T(8,128)} %get-tuple-element.100) | copy-start | bytes 1769476
  209.0 4.7 %copy-start.17 = (pred[2304]{0:T(1024)(128)(4,1)S(1)}, pred[2304]{0:T(1024)(128)(4,1)}, u32[]{:S(2)}) copy-start(pred[2304]{0:T(1024)(128)(4,1)} %dynamic-slice_reduce_fusion) | copy-start | bytes 6916
  209.1 4.7 %copy-start.18 = (pred[2304]{0:T(1024)(128)(4,1)S(1)}, pred[2304]{0:T(1024)(128)(4,1)}, u32[]{:S(2)}) copy-start(pred[2304]{0:T(1024)(128)(4,1)} %and_reduce_fusion) | copy-start | bytes 6916
  239.5 9.4 %copy-start.3 = (bf16[1,2304,128]{2,1,0:T(8,128)(2,1)S(1)}, bf16[1,2304,128]{2,1,0:T(8,128)(2,1)}, u32[]{:S(2)}) copy-start(bf16[1,2304,128]{2,1,0:T(8,128)(2,1)} %get-tuple-element.204) | copy-start | bytes 1769476
  240.5 34.2 %all-to-all-start.4 = ((bf16[32,2,4608]{2,1,0:T(2,128)(2,1)}), bf16[32,2,4608]{2,1,0:T(2,128)(2,1)S(1)}, u32[]{:S(2)}, u32[]{:S(2)}) async-start(bf16[32,2,4608]{2,1,0:T(2,128)(2,1)} %reshape.594), calls=%async_computation.4 | async-start | bytes 1179648 | tf_op jit(solution)/shard_map/all_to_all | solution.py:163
  272.1 12.2 %copy-start.2 = (bf16[1,2304,128]{2,1,0:T(8,128)(2,1)S(1)}, bf16[1,2304,128]{2,1,0:T(8,128)(2,1)}, u32[]{:S(2)}) copy-start(bf16[1,2304,128]{2,1,0:T(8,128)(2,1)} %get-tuple-element.205) | copy-start | bytes 1769476
  274.7 32.9 %all-to-all-start.5 = ((bf16[32,2,4608]{2,1,0:T(2,128)(2,1)}), bf16[32,2,4608]{2,1,0:T(2,128)(2,1)}, u32[]{:S(2)}, u32[]{:S(2)}) async-start(bf16[32,2,4608]{2,1,0:T(2,128)(2,1)} %reshape.596), calls=%async_computation.5 | async-start | bytes 1179648 | tf_op jit(solution)/shard_map/all_to_all | solution.py:164
  307.7 32.2 %all-to-all-start.6 = ((bf16[32,2,4608]{2,1,0:T(2,128)(2,1)}), bf16[32,2,4608]{2,1,0:T(2,128)(2,1)S(1)}, u32[]{:S(2)}, u32[]{:S(2)}) async-start(bf16[32,2,4608]{2,1,0:T(2,128)(2,1)} %reshape.598), calls=%async_computation.6 | async-start | bytes 1179648 | tf_op jit(solution)/shard_map/all_to_all | solution.py:165
  339.9 126.8 %all-to-all-start.7 = ((bf16[32,2,4608]{2,1,0:T(2,128)(2,1)}), bf16[32,2,4608]{2,1,0:T(2,128)(2,1)S(1)}, u32[]{:S(2)}, u32[]{:S(2)}) async-start(bf16[32,2,4608]{2,1,0:T(2,128)(2,1)} %reshape.600), calls=%async_computation.7 | async-start | bytes 1179648 | tf_op jit(solution)/shard_map/all_to_all | solution.py:166
  (33 other events, 47.8 us)
where the time goes:
time: 472 us; the launch traced here: 468 us
  blocking collectives  138 us (29%)
  local copies, waits for them, and re-layouts  129 us (27%)
  other arithmetic  76.4 us (16%)
  starting transfers between devices  57.5 us (12%)
  matrix products  42.1 us (9%)
  waiting for transfers between devices  16.7 us (4%)
  loops' own time  6.58 us (1%)
    psum x1, blocking collectives, body(): gain_grad = lax.psum(jnp.sum(gain_part, axis=0), ('ctx', 'dp'))  110 us
    unnamed x6, other arithmetic  52.5 us
    select_n x4, local copies, waits for them, and re-layouts, spread(): return jnp.where(home_mask[:, :, None], taken, jnp.zeros((), jnp.bfloat16))  37.8 us
    all_to_all x1, blocking collectives, body(): lax.all_to_all(queries.reshape(pair_count, shard_len, head_dim), 'ctx', s...  28 us
    dot_general x18, matrix products, dot_first(): lax.dot_general(left, right, (((0,), (0,)), ((), ())), preferred_element_...  24.2 us
    gather x3, local copies, waits for them, and re-layouts, body(): jnp.take_along_axis(keep_order.reshape(samples, devices * shard_len), sou...  19 us
    gather x4, local copies, waits for them, and re-layouts, body(): within = ranks[None, :] - jnp.take_along_axis(starting, source, axis=1)  18.8 us
    gather x4, local copies, waits for them, and re-layouts, spread(): taken = jnp.take_along_axis(result, home_index[:, :, None], axis=1)  18.7 us
  transfers between devices with their start and end apart: 7, of which 2 were waited for; matrix products, arithmetic and copies ran while one was open for 28% of the time, Pallas kernels for 0%

commit v1 on v0

v1 whole, which is shorter than its diff:
```python
import jax
import jax.numpy as jnp
from jax import lax
from jax.experimental import pallas as pl
from jax.experimental.pallas import tpu as pltpu
from jax.sharding import PartitionSpec as P

EPS = 1e-06
MESH = pl.DeviceIdType.MESH
BF = jnp.bfloat16
F32 = jnp.float32

DEV = 32
DP = 16
HEADS = 16
TS = 72
HD = 128
KEPT = 1152
MSG = 112
MAIN = 48
HALF = 64
WIDE = DEV * HALF
PAD = KEPT + 64
BLK = 128
BIG = 384


def dot(left, right):
    return jnp.dot(left, right, preferred_element_type=F32)


def dot_last(left, right):
    return lax.dot_general(left, right, (((1,), (1,)), ((), ())), preferred_element_type=F32)


def iota(shape, dim):
    return lax.broadcasted_iota(jnp.int32, shape, dim)


def loop(lo, hi, step, unroll=1):
    def run(index, carry):
        step(index)
        return carry

    lax.fori_loop(lo, hi, run, 0, unroll=unroll)


def kernel(
    gains, order, count_v, count_s, q_hbm, k_hbm, v_hbm, g_hbm,
    o_hbm, dq_hbm, dk_hbm, dv_hbm, gain_out,
    xs, outs, send_qk, send_vg, recv_qk, recv_vg, send_ov, send_dd, recv_ov, recv_dd,
    pack_a, pack_b, unpack, hot_a, hot_b, place_a, place_b,
    prob, prob_b, ds_b, qn, kn, vv, gg, uq, uk, iq, ik, qn_t, gg_t,
    y_o, y_dv, y_dq, y_dk, gsend, gbuf, hsend, hbuf, starts,
    in_sem, out_sem, fs, fr, bs, br, dds, ddr, gs, gr,
):
    me = lax.axis_index("ctx")
    dp = lax.axis_index("dp")
    own_sample = me // HEADS
    scale = HD ** (-0.5)

    def ahead(k):
        return lax.rem(me + k, DEV)

    def behind(k):
        return lax.rem(me + DEV - k, DEV)

    barrier = pltpu.get_barrier_semaphore()
    loop(1, DEV, lambda k: pl.semaphore_signal(
        barrier, inc=1, device_id={"ctx": ahead(k)}, device_id_type=MESH))
    loop(1, DP, lambda k: pl.semaphore_signal(
        barrier, inc=1, device_id={"dp": lax.rem(dp + k, DP)}, device_id_type=MESH))

    loads = [
        pltpu.make_async_copy(ref, xs.at[i], in_sem.at[i])
        for i, ref in enumerate((q_hbm, k_hbm, v_hbm, g_hbm))
    ]
    for load in loads:
        load.start()

    row, slot = iota((MSG, TS), 0), iota((MSG, TS), 1)
    pick_a = ((row == slot) & (row < 54)).astype(F32).astype(BF)
    pick_b = (
        ((row >= HALF) & (slot == row - HALF)) | ((row >= 56) & (row < 62) & (slot == row - 8))
    ).astype(F32).astype(BF)
    for s in range(2):
        tokens = order[s, pl.ds(me, 1), :]
        own_count = count_s[s, me]
        chosen = ((iota((TS, TS), 0) == tokens) & (iota((TS, TS), 1) < own_count))
        chosen = chosen.astype(F32).astype(BF)
        pack_a[s] = dot_last(pick_a, chosen).astype(BF)
        pack_b[s] = dot_last(pick_b, chosen).astype(BF)
        unpack[s, 0:TS] = dot_last(chosen, pick_a).astype(BF)
        unpack[s, TS : 2 * TS] = dot_last(chosen, pick_b).astype(BF)

    for load in loads:
        load.wait()

    def packed(k):
        pair = ahead(k)
        s = pair // HEADS
        first = jnp.concatenate([xs[0, pair], xs[2, pair]], axis=1)
        second = jnp.concatenate([xs[1, pair], xs[3, pair]], axis=1)
        rows = (dot(pack_a[s], first) + dot(pack_b[s], second)).astype(BF)
        return rows[:, :HD], rows[:, HD:]

    recv_qk[0], recv_vg[0] = packed(0)

    def pack(k):
        send_qk[k], send_vg[k] = packed(k)

    loop(1, DEV, pack)
    pl.semaphore_wait(barrier, DEV - 1 + DP - 1)

    def remote(src, dst, send_sem, recv_sem, peer):
        return pltpu.make_async_remote_copy(
            src_ref=src, dst_ref=dst, send_sem=send_sem, recv_sem=recv_sem,
            device_id={"ctx": peer}, device_id_type=MESH)

    def part(src, dst, which, lo, size, sems, semr, peer):
        rows = pl.ds(lo, size)
        return remote(
            src.at[which, rows], dst.at[which, rows], sems, semr, peer
        )

    every = pl.ds(1, DEV - 1)

    def fwd_qk(k):
        return part(send_qk, recv_qk, k, 0, MSG, fs.at[0], fr.at[0], ahead(1))

    loop(1, DEV, lambda k: part(
        send_qk, recv_qk, k, 0, MSG, fs.at[0], fr.at[0], ahead(k)).start())
    loop(1, DEV, lambda k: part(
        send_vg, recv_vg, k, 0, HALF, fs.at[1], fr.at[1], ahead(k)).start())
    loop(1, DEV, lambda k: part(
        send_vg, recv_vg, k, HALF, MAIN, fs.at[2], fr.at[2], ahead(k)).start())
    all_qk = part(send_qk, recv_qk, every, 0, MSG, fs.at[0], fr.at[0], ahead(1))
    all_v = part(send_vg, recv_vg, every, 0, HALF, fs.at[1], fr.at[1], ahead(1))
    all_g = part(send_vg, recv_vg, every, HALF, MAIN, fs.at[2], fr.at[2], ahead(1))

    def add_start(c, total):
        starts[c] = total
        return total + count_s[own_sample, c]

    lax.fori_loop(0, DEV, add_start, jnp.int32(0))
    counts = count_v[pl.ds(own_sample, 1), :].astype(F32)
    upto = (iota((DEV, DEV), 0) <= iota((DEV, DEV), 1)).astype(F32).astype(BF)
    ends = dot(jnp.broadcast_to(counts, (8, DEV)).astype(BF), upto)[0:1, :]
    ranks = iota((KEPT, DEV), 0).astype(F32)
    past = ends <= ranks
    shard = jnp.sum(jnp.where(past, 1.0, 0.0), axis=1, keepdims=True)
    start = jnp.sum(jnp.where(past, counts, 0.0), axis=1, keepdims=True)
    within = iota((KEPT, 1), 0).astype(F32) - start
    place = me.astype(F32) - shard
    place = jnp.where(place < 0.0, place + DEV, place) * HALF
    at_a = (place + within).astype(jnp.int32)
    at_b = (place + jnp.where(within < MAIN, within + 16.0, within - 40.0)).astype(jnp.int32)
    place_a[...] = jnp.broadcast_to(at_a, (KEPT, HD))
    place_b[...] = jnp.broadcast_to(at_b, (KEPT, HD))

    def fill(b):
        rows = pl.ds(pl.multiple_of(b * BLK, BLK), BLK)
        lane = iota((BLK, HD), 1)
        for where, hot in ((place_a, hot_a), (place_b, hot_b)):
            at = where[rows] - lane
            for n in range(WIDE // HD):
                hot[rows, n * HD : (n + 1) * HD] = (at == n * HD).astype(F32).astype(BF)

    loop(0, KEPT // BLK, fill)
    for y in (y_o, y_dv, y_dq, y_dk):
        y[KEPT:PAD] = jnp.zeros((PAD - KEPT, HD), F32)

    def big(b):
        return pl.ds(pl.multiple_of(b * BIG, BIG), BIG)

    def gather(hot, rows, recv, lo):
        return dot(hot[rows], recv[:, lo : lo + HALF].reshape(WIDE, HD))

    all_qk.wait_recv()

    def norms(b):
        rows = big(b)
        for hot, lo, unit_ref, inv_ref, norm_ref, i in (
            (hot_a, 0, uq, iq, qn, 0),
            (hot_b, MAIN, uk, ik, kn, 1),
        ):
            x = gather(hot, rows, recv_qk, lo)
            inv = lax.rsqrt(jnp.mean(x * x, axis=-1, keepdims=True) + EPS)
            unit = x * inv
            unit_ref[rows] = unit
            inv_ref[rows] = jnp.broadcast_to(inv, (BIG, HD))
            norm_ref[rows] = (unit * gains[i : i + 1, :]).astype(BF)

    loop(0, KEPT // BIG, norms)
    qn_t[...] = jnp.transpose(qn[...].astype(F32)).astype(BF)

    def softmax(b):
        rows = pl.ds(pl.multiple_of(b * BLK, BLK), BLK)
        scores = dot_last(qn[rows], kn[...]) * scale
        peak = jnp.max(scores, axis=-1, keepdims=True)
        expo = jnp.exp(scores - peak)
        p = expo / jnp.sum(expo, axis=-1, keepdims=True)
        prob[rows] = p
        prob_b[rows] = p.astype(BF)

    loop(0, KEPT // BLK, softmax)

    all_v.wait_recv()

    def attend(b):
        vv[big(b)] = gather(hot_a, big(b), recv_vg, 0).astype(BF)

    loop(0, KEPT // BIG, attend)

    def attend2(b):
        y_o[big(b)] = dot(prob_b[big(b)], vv[...])

    loop(0, KEPT // BIG, attend2)

    def main_rows(y, k):
        return y[pl.ds(starts[behind(k)], MAIN), :].astype(BF)

    def tail_rows(y, z, k):
        at = pl.ds(starts[behind(k)] + MAIN, 8)
        return jnp.concatenate([y[at, :], z[at, :]], axis=0).astype(BF)

    recv_ov[0, 0:MAIN] = main_rows(y_o, 0)

    def out_main(k):
        send_ov[k, 0:MAIN] = main_rows(y_o, k)

    loop(1, DEV, out_main)
    all_g.wait_send()
    loop(1, DEV, lambda k: part(
        send_ov, recv_ov, k, 0, MAIN, bs.at[0], br.at[0], behind(k)).start())
    all_o = part(send_ov, recv_ov, every, 0, MAIN, bs.at[0], br.at[0], behind(1))

    all_g.wait_recv()

    def cotangents(b):
        gg[big(b)] = gather(hot_b, big(b), recv_vg, MAIN).astype(BF)

    loop(0, KEPT // BIG, cotangents)
    gg_t[...] = jnp.transpose(gg[...].astype(F32)).astype(BF)

    def column(b):
        return pl.ds(pl.multiple_of(b * BIG, BIG), BIG)

    def value_back(b):
        y_dv[big(b)] = jnp.transpose(dot(gg_t[...], prob_b[:, column(b)]))

    loop(0, KEPT // BIG, value_back)
    recv_ov[0, MAIN:HALF] = tail_rows(y_o, y_dv, 0)
    recv_ov[0, HALF:MSG] = main_rows(y_dv, 0)

    def value_main(k):
        send_ov[k, MAIN:HALF] = tail_rows(y_o, y_dv, k)
        send_ov[k, HALF:MSG] = main_rows(y_dv, k)
        part(send_ov, recv_ov, k, MAIN, HALF, bs.at[1], br.at[1], behind(k)).start()

    loop(1, DEV, value_main)
    all_dv = part(send_ov, recv_ov, every, MAIN, HALF, bs.at[1], br.at[1], behind(1))

    def score_back(b):
        rows = pl.ds(pl.multiple_of(b * BLK, BLK), BLK)
        dprob = dot_last(gg[rows], vv[...])
        p = prob[rows]
        delta = jnp.sum(p * dprob, axis=-1, keepdims=True)
        ds_b[rows] = (p * (dprob - delta)).astype(BF)

    loop(0, KEPT // BLK, score_back)

    def norm_back(grad, rows, unit_ref, inv_ref, i, y):
        unit = unit_ref[rows]
        tangent = grad * gains[i : i + 1, :]
        y[rows] = inv_ref[rows] * (
            tangent - unit * jnp.mean(tangent * unit, axis=-1, keepdims=True)
        )
        gsend[i : i + 1, :] += jnp.sum(grad * unit, axis=0, keepdims=True)

    gsend[...] = jnp.zeros_like(gsend)

    def query_back(b):
        grad = dot(ds_b[big(b)], kn[...]) * scale
        norm_back(grad, big(b), uq, iq, 0, y_dq)

    loop(0, KEPT // BIG, query_back)

    def key_back(b):
        grad = jnp.transpose(dot(qn_t[...], ds_b[:, column(b)])) * scale
        norm_back(grad, big(b), uk, ik, 1, y_dk)

    loop(0, KEPT // BIG, key_back)

    def gain_ctx(k):
        return remote(gsend, gbuf.at[k], gs.at[0], gr.at[0], ahead(k))

    gbuf[0] = gsend[...]
    loop(1, DEV, lambda k: gain_ctx(k).start())

    def grad_rows(k):
        return main_rows(y_dq, k), tail_rows(y_dq, y_dk, k), main_rows(y_dk, k)

    recv_dd[0, 0:MAIN], recv_dd[0, MAIN:HALF], recv_dd[0, HALF:MSG] = grad_rows(0)

    def back_dd(k):
        return part(send_dd, recv_dd, k, 0, MSG, dds, ddr.at[k], behind(k))

    def grad_main(k):
        send_dd[k, 0:MAIN], send_dd[k, MAIN:HALF], send_dd[k, HALF:MSG] = grad_rows(k)
        back_dd(k).start()

    loop(1, DEV, grad_main)
    all_dd = part(send_dd, recv_dd, every, 0, MSG, dds, ddr.at[0], behind(1))

    gain_all = pltpu.make_async_remote_copy(
        src_ref=gbuf.at[every], dst_ref=gbuf.at[every], send_sem=gs.at[0], recv_sem=gr.at[0],
        device_id={"ctx": ahead(1)}, device_id_type=MESH)
    gain_all.wait_recv()
    hsend[...] = lax.fori_loop(
        0, DEV, lambda c, acc: acc + gbuf[behind(c)], jnp.zeros((8, HD), F32)
    )
    hbuf[0] = hsend[...]

    def gain_dp(k):
        return pltpu.make_async_remote_copy(
            src_ref=hsend, dst_ref=hbuf.at[k], send_sem=gs.at[1], recv_sem=gr.at[1],
            device_id={"dp": lax.rem(dp + k, DP)}, device_id_type=MESH)

    loop(1, DP, lambda k: gain_dp(k).start())
    others = pl.ds(1, DP - 1)
    gain_dps = pltpu.make_async_remote_copy(
        src_ref=hbuf.at[others], dst_ref=hbuf.at[others], send_sem=gs.at[1], recv_sem=gr.at[1],
        device_id={"dp": lax.rem(dp + 1, DP)}, device_id_type=MESH)

    all_o.wait_recv()
    all_dv.wait_recv()

    def home(k, recv, first, second):
        pair = ahead(k)
        rows = dot(unpack[pair // HEADS], recv[k]).astype(BF)
        outs[first, pair] = rows[:TS]
        outs[second, pair] = rows[TS:]

    loop(0, DEV, lambda k: home(k, recv_ov, 0, 3))
    stores = [
        pltpu.make_async_copy(outs.at[i], ref, out_sem.at[i])
        for i, ref in enumerate((o_hbm, dq_hbm, dk_hbm, dv_hbm))
    ]
    stores[0].start()
    stores[3].start()
    gain_dps.wait_recv()
    total = lax.fori_loop(
        0, DP, lambda c, acc: acc + hbuf[lax.rem(dp + DP - c, DP)], jnp.zeros((8, HD), F32)
    )
    gain_out[...] = total[0:2]
    home(0, recv_dd, 1, 2)

    def last(k):
        back_dd(k).wait_recv()
        home(k, recv_dd, 1, 2)

    loop(1, DEV, last)
    stores[1].start()
    stores[2].start()
    all_qk.wait_send()
    all_v.wait_send()
    all_o.wait_send()
    all_dv.wait_send()
    all_dd.wait_send()
    gain_all.wait_send()
    gain_dps.wait_send()
    for store in stores:
        store.wait()


def body(queries, keys, values, out_grad, gains, keep_order, keep_count):
    pairs = [x.reshape(DEV, TS, HD) for x in (queries, keys, values, out_grad)]
    vmem = pl.BlockSpec(memory_space=pltpu.VMEM)
    smem = pl.BlockSpec(memory_space=pltpu.SMEM)
    hbm = pl.BlockSpec(memory_space=pl.ANY)
    message = pltpu.VMEM((DEV, MSG, HD), BF)
    rows_b, rows_f = pltpu.VMEM((KEPT, HD), BF), pltpu.VMEM((KEPT, HD), F32)
    result = pltpu.VMEM((PAD, HD), F32)
    place = pltpu.VMEM((KEPT, HD), jnp.int32)
    hot = pltpu.VMEM((KEPT, WIDE), BF)
    square_f, square_b = pltpu.VMEM((KEPT, KEPT), F32), pltpu.VMEM((KEPT, KEPT), BF)
    turned = pltpu.VMEM((HD, KEPT), BF)
    dma = pltpu.SemaphoreType.DMA
    out = jax.ShapeDtypeStruct((DEV, TS, HD), BF)
    results = pl.pallas_call(
        kernel,
        out_shape=[out] * 4 + [jax.ShapeDtypeStruct((2, HD), F32)],
        in_specs=[vmem, vmem, vmem, smem] + [hbm] * 4,
        out_specs=[hbm] * 4 + [vmem],
        scratch_shapes=[pltpu.VMEM((4, DEV, TS, HD), BF)] * 2
        + [message] * 8
        + [pltpu.VMEM((2, MSG, TS), BF)] * 2
        + [pltpu.VMEM((2, 2 * TS, MSG), BF)]
        + [hot] * 2
        + [place] * 2
        + [square_f, square_b, square_b]
        + [rows_b] * 4
        + [rows_f] * 4
        + [turned] * 2
        + [result] * 4
        + [pltpu.VMEM((8, HD), F32), pltpu.VMEM((DEV, 8, HD), F32)]
        + [pltpu.VMEM((8, HD), F32), pltpu.VMEM((DP, 8, HD), F32)]
        + [pltpu.SMEM((DEV,), jnp.int32)]
        + [dma((4,)), dma((4,)), dma((3,)), dma((3,)), dma((2,)), dma((2,))]
        + [dma, dma((DEV,)), dma((2,)), dma((2,))],
        compiler_params=pltpu.CompilerParams(
            collective_id=0, has_side_effects=True, vmem_limit_bytes=60 * 1024 * 1024
        ),
    )(gains, keep_order, keep_count, keep_count, *pairs)
    shape = queries.shape
    return tuple(r.reshape(shape) for r in results[:4]) + (results[4],)


def solution(mesh):
    rows = P("dp", None, "ctx", None)
    return jax.shard_map(
        body,
        mesh=mesh,
        in_specs=(rows, rows, rows, rows, P(), P("dp", None, None), P("dp", None)),
        out_specs=(rows, rows, rows, rows, P()),
        check_vma=False,
    )
```

time: 472 us -> 112 us (0.24)
  blocking collectives: 138 us -> 0 us
  local copies, waits for them, and re-layouts: 129 us -> 5.92 us
  Pallas kernels: 0 us -> 104 us
  other arithmetic: 76.4 us -> 0 us
  starting transfers between devices: 57.5 us -> 0 us
  matrix products: 42.1 us -> 0 us
  waiting for transfers between devices: 16.7 us -> 0 us
  loops' own time: 6.58 us -> 0 us
    psum x1 -> x0, blocking collectives: 110 us -> none  [body(): gain_grad = lax.psum(jnp.sum(gain_part, axis=0), ('ctx', 'dp'))]
    pallas_call x0 -> x1, Pallas kernels: none -> 104 us  [body(): pl.pallas_call(kernel, out_shape=[out] * 4 + [jax.ShapeDtypeStruct((2, HD...]
    gather x16 -> x0, local copies, waits for them, and re-layouts: 70 us -> none  [the longest x3 19 us: body(): jnp.take_along_axis(keep_order.reshape(samples, devices * shard_len), sou...]
    all_to_all x7 -> x0, starting transfers between devices: 57.5 us -> none  [the longest x1 9.59 us: body(): lax.all_to_all(spread(query_grad), 'ctx', split_axis=1, concat_axis=0, ti...]
    unnamed x6 -> x0, other arithmetic: 52.5 us -> none
    dot_general x54 -> x0, matrix products: 42.1 us -> none  [the longest x18 24.2 us: dot_first(): lax.dot_general(left, right, (((0,), (0,)), ((), ())), preferred_element_...]
    select_n x4 -> x0, local copies, waits for them, and re-layouts: 37.8 us -> none  [spread(): return jnp.where(home_mask[:, :, None], taken, jnp.zeros((), jnp.bfloat16))]
    all_to_all x1 -> x0, blocking collectives: 28 us -> none  [body(): lax.all_to_all(queries.reshape(pair_count, shard_len, head_dim), 'ctx', s...]
  transfers between devices with their start and end apart: 7 -> 0, of which waited for: 2 -> 0; matrix products, arithmetic and copies ran while one was open for 28% -> 0% of each run, Pallas kernels for 0% -> 0%
where the time goes in v1:
time: 112 us; the launch traced here: 110 us
  Pallas kernels  104 us (93%)
  local copies, waits for them, and re-layouts  5.92 us (5%)
    pallas_call x1, Pallas kernels, body(): pl.pallas_call(kernel, out_shape=[out] * 4 + [jax.ShapeDtypeStruct((2, HD...  104 us
    unnamed x13, local copies, waits for them, and re-layouts  5.92 us

profile of v1, /device:TPU:1, one launch (start us, length us, event | category | flops | bytes accessed | tf_op | source)
XLA Modules:
  0.0 110.3 jit_solution(5252771315719170819)
XLA Ops:
  0.6 103.7 %shard_map.110 = (bf16[32,72,128]{2,1,0:T(8,128)(2,1)}, bf16[32,72,128]{2,1,0:T(8,128)(2,1)}, bf16[32,72,128]{2,1,0:T(8,128)(2,1)}, bf16[32,72,128]{2,1,0:T(8,128)(2,1)}, f32[2,128]{1,0:T(2,128)}) custom-call(f32[2,128]{1,0:T(2,128)} %gains.1, s32[2,32,72]{2,1,0:T(8,128)} %order.1, s32[2,32]{1,0:T(2,128)} %count_s.1, s32[2,32]{1,0:T(2,128)} %count_s.1, ...), custom_call_target="tpu_custom_call" | custom-call | tf_op jit(solution)/shard_map/pallas_call | solution.py:391
  104.4 0.0 copy-start.2
  104.4 2.0 %copy.17 = bf16[2,16,72,128]{3,2,1,0:T(8,128)(2,1)} copy(bf16[2,16,72,128]{3,2,1,0:T(8,128)(2,1)} %bitcast.15) | data formatting | bytes 1179648
  106.4 0.0 copy-done.2
  106.4 0.0 copy-start.1
  106.4 0.8 copy.18
  107.2 0.5 copy-done.1
  107.7 0.0 copy-start
  107.7 0.8 copy.19
  108.5 0.5 copy-done
  108.9 0.0 copy-start.3
  108.9 0.8 copy.20
  109.8 0.0 copy-done.3
  109.8 0.6 copy.21
Async XLA Ops:
  104.4 2.0 %copy-start.2 = (bf16[32,72,128]{2,1,0:T(8,128)(2,1)S(1)}, bf16[32,72,128]{2,1,0:T(8,128)(2,1)}, u32[]{:S(2)}) copy-start(bf16[32,72,128]{2,1,0:T(8,128)(2,1)} %get-tuple-element.11) | copy-start | bytes 1769476
  106.4 1.3 %copy-start.1 = (bf16[32,72,128]{2,1,0:T(8,128)(2,1)S(1)}, bf16[32,72,128]{2,1,0:T(8,128)(2,1)}, u32[]{:S(2)}) copy-start(bf16[32,72,128]{2,1,0:T(8,128)(2,1)} %get-tuple-element.12) | copy-start | bytes 1769476
  107.7 1.3 %copy-start = (bf16[32,72,128]{2,1,0:T(8,128)(2,1)S(1)}, bf16[32,72,128]{2,1,0:T(8,128)(2,1)}, u32[]{:S(2)}) copy-start(bf16[32,72,128]{2,1,0:T(8,128)(2,1)} %get-tuple-element.13) | copy-start | bytes 1769476
  108.9 0.8 copy-start.3

commit v2 on v1

--- a/solution.py
+++ b/solution.py
@@ -47,12 +47,12 @@
 
 def kernel(
     gains, order, count_v, count_s, q_hbm, k_hbm, v_hbm, g_hbm,
-    o_hbm, dq_hbm, dk_hbm, dv_hbm, gain_out,
-    xs, outs, send_qk, send_vg, recv_qk, recv_vg, send_ov, send_dd, recv_ov, recv_dd,
+    outs, gain_out,
+    xs, send_qk, send_vg, recv_qk, recv_vg, send_ov, send_dd, recv_ov, recv_dd,
     pack_a, pack_b, unpack, hot_a, hot_b, place_a, place_b,
     prob, prob_b, ds_b, qn, kn, vv, gg, uq, uk, iq, ik, qn_t, gg_t,
-    y_o, y_dv, y_dq, y_dk, gsend, gbuf, hsend, hbuf, starts,
-    in_sem, out_sem, fs, fr, bs, br, dds, ddr, gs, gr,
+    y_o, y_dv, y_dq, y_dk, gsend, gbuf, hsend, hbuf, total, starts,
+    in_sem, fs, fr, bs, br, dds, ddr, gs, gr,
 ):
     me = lax.axis_index("ctx")
     dp = lax.axis_index("dp")
@@ -65,11 +65,23 @@
     def behind(k):
         return lax.rem(me + DEV - k, DEV)
 
+    def spread(step):
+        def both(k):
+            step(k)
+            step(DEV - k)
+
+        loop(1, DEV // 2, both)
+        step(DEV // 2)
+
+    is_hub = me == 0
     barrier = pltpu.get_barrier_semaphore()
     loop(1, DEV, lambda k: pl.semaphore_signal(
         barrier, inc=1, device_id={"ctx": ahead(k)}, device_id_type=MESH))
-    loop(1, DP, lambda k: pl.semaphore_signal(
-        barrier, inc=1, device_id={"dp": lax.rem(dp + k, DP)}, device_id_type=MESH))
+
+    @pl.when(is_hub)
+    def _():
+        loop(1, DP, lambda k: pl.semaphore_signal(
+            barrier, inc=1, device_id={"dp": lax.rem(dp + k, DP)}, device_id_type=MESH))
 
     loads = [
         pltpu.make_async_copy(ref, xs.at[i], in_sem.at[i])
@@ -110,7 +122,14 @@
         send_qk[k], send_vg[k] = packed(k)
 
     loop(1, DEV, pack)
-    pl.semaphore_wait(barrier, DEV - 1 + DP - 1)
+
+    @pl.when(is_hub)
+    def _():
+        pl.semaphore_wait(barrier, DEV - 1 + DP - 1)
+
+    @pl.when(jnp.logical_not(is_hub))
+    def _():
+        pl.semaphore_wait(barrier, DEV - 1)
 
     def remote(src, dst, send_sem, recv_sem, peer):
         return pltpu.make_async_remote_copy(
@@ -125,14 +144,11 @@
 
     every = pl.ds(1, DEV - 1)
 
-    def fwd_qk(k):
-        return part(send_qk, recv_qk, k, 0, MSG, fs.at[0], fr.at[0], ahead(1))
-
-    loop(1, DEV, lambda k: part(
+    spread(lambda k: part(
         send_qk, recv_qk, k, 0, MSG, fs.at[0], fr.at[0], ahead(k)).start())
-    loop(1, DEV, lambda k: part(
+    spread(lambda k: part(
         send_vg, recv_vg, k, 0, HALF, fs.at[1], fr.at[1], ahead(k)).start())
-    loop(1, DEV, lambda k: part(
+    spread(lambda k: part(
         send_vg, recv_vg, k, HALF, MAIN, fs.at[2], fr.at[2], ahead(k)).start())
     all_qk = part(send_qk, recv_qk, every, 0, MSG, fs.at[0], fr.at[0], ahead(1))
     all_v = part(send_vg, recv_vg, every, 0, HALF, fs.at[1], fr.at[1], ahead(1))
@@ -231,7 +247,7 @@
 
     loop(1, DEV, out_main)
     all_g.wait_send()
-    loop(1, DEV, lambda k: part(
+    spread(lambda k: part(
         send_ov, recv_ov, k, 0, MAIN, bs.at[0], br.at[0], behind(k)).start())
     all_o = part(send_ov, recv_ov, every, 0, MAIN, bs.at[0], br.at[0], behind(1))
 
@@ -258,7 +274,7 @@
         send_ov[k, HALF:MSG] = main_rows(y_dv, k)
         part(send_ov, recv_ov, k, MAIN, HALF, bs.at[1], br.at[1], behind(k)).start()
 
-    loop(1, DEV, value_main)
+    spread(value_main)
     all_dv = part(send_ov, recv_ov, every, MAIN, HALF, bs.at[1], br.at[1], behind(1))
 
     def score_back(b):
@@ -292,11 +308,37 @@
 
     loop(0, KEPT // BIG, key_back)
 
-    def gain_ctx(k):
-        return remote(gsend, gbuf.at[k], gs.at[0], gr.at[0], ahead(k))
-
-    gbuf[0] = gsend[...]
-    loop(1, DEV, lambda k: gain_ctx(k).start())
+    to_hub = remote(gsend, gbuf.at[me], gs.at[0], gr.at[0], 0)
+    from_devs = remote(gbuf.at[every], gbuf.at[every], gs.at[0], gr.at[0], 0)
+    others = pl.ds(1, DP - 1)
+
+    def to_group(k):
+        return remote(total.at[0], total.at[1], gs.at[2], gr.at[2], ahead(k))
+
+    def between(src, dst, k):
+        return pltpu.make_async_remote_copy(
+            src_ref=src, dst_ref=dst, send_sem=gs.at[1], recv_sem=gr.at[1],
+            device_id={"dp": lax.rem(dp + k, DP)}, device_id_type=MESH)
+
+    @pl.when(jnp.logical_not(is_hub))
+    def _():
+        to_hub.start()
+
+    @pl.when(is_hub)
+    def _():
+        gbuf[0] = gsend[...]
+        from_devs.wait_recv()
+        hsend[...] = lax.fori_loop(
+            0, DEV, lambda c, acc: acc + gbuf[c], jnp.zeros((8, HD), F32)
+        )
+        hbuf[0] = hsend[...]
+        loop(1, DP, lambda k: between(hsend, hbuf.at[k], k).start())
+        between(hbuf.at[others], hbuf.at[others], 1).wait_recv()
+        total[0] = lax.fori_loop(
+            0, DP, lambda c, acc: acc + hbuf[lax.rem(dp + DP - c, DP)], jnp.zeros((8, HD), F32)
+        )
+        total[1] = total[0]
+        loop(1, DEV, lambda k: to_group(k).start())
 
     def grad_rows(k):
         return main_rows(y_dq, k), tail_rows(y_dq, y_dk, k), main_rows(y_dk, k)
@@ -310,28 +352,8 @@
         send_dd[k, 0:MAIN], send_dd[k, MAIN:HALF], send_dd[k, HALF:MSG] = grad_rows(k)
         back_dd(k).start()
 
-    loop(1, DEV, grad_main)
+    spread(grad_main)
     all_dd = part(send_dd, recv_dd, every, 0, MSG, dds, ddr.at[0], behind(1))
-
-    gain_all = pltpu.make_async_remote_copy(
-        src_ref=gbuf.at[every], dst_ref=gbuf.at[every], send_sem=gs.at[0], recv_sem=gr.at[0],
-        device_id={"ctx": ahead(1)}, device_id_type=MESH)
-    gain_all.wait_recv()
-    hsend[...] = lax.fori_loop(
-        0, DEV, lambda c, acc: acc + gbuf[behind(c)], jnp.zeros((8, HD), F32)
-    )
-    hbuf[0] = hsend[...]
-
-    def gain_dp(k):
-        return pltpu.make_async_remote_copy(
-            src_ref=hsend, dst_ref=hbuf.at[k], send_sem=gs.at[1], recv_sem=gr.at[1],
-            device_id={"dp": lax.rem(dp + k, DP)}, device_id_type=MESH)
-
-    loop(1, DP, lambda k: gain_dp(k).start())
-    others = pl.ds(1, DP - 1)
-    gain_dps = pltpu.make_async_remote_copy(
-        src_ref=hbuf.at[others], dst_ref=hbuf.at[others], send_sem=gs.at[1], recv_sem=gr.at[1],
-        device_id={"dp": lax.rem(dp + 1, DP)}, device_id_type=MESH)
 
     all_o.wait_recv()
     all_dv.wait_recv()
@@ -343,35 +365,42 @@
         outs[second, pair] = rows[TS:]
 
     loop(0, DEV, lambda k: home(k, recv_ov, 0, 3))
-    stores = [
-        pltpu.make_async_copy(outs.at[i], ref, out_sem.at[i])
-        for i, ref in enumerate((o_hbm, dq_hbm, dk_hbm, dv_hbm))
-    ]
-    stores[0].start()
-    stores[3].start()
-    gain_dps.wait_recv()
-    total = lax.fori_loop(
-        0, DP, lambda c, acc: acc + hbuf[lax.rem(dp + DP - c, DP)], jnp.zeros((8, HD), F32)
-    )
-    gain_out[...] = total[0:2]
     home(0, recv_dd, 1, 2)
 
     def last(k):
         back_dd(k).wait_recv()
         home(k, recv_dd, 1, 2)
 
-    loop(1, DEV, last)
-    stores[1].start()
-    stores[2].start()
+    spread(last)
+
+    @pl.when(is_hub)
+    def _():
+        between(hbuf.at[others], hbuf.at[others], 1).wait_send()
+        loop(1, DEV, lambda k: to_group(k).wait_send())
+
+    @pl.when(jnp.logical_not(is_hub))
+    def _():
+        to_hub.wait_send()
+        to_group(1).wait_recv()
+
+    gain_out[...] = total[1, 0:2]
     all_qk.wait_send()
     all_v.wait_send()
     all_o.wait_send()
     all_dv.wait_send()
     all_dd.wait_send()
-    gain_all.wait_send()
-    gain_dps.wait_send()
-    for store in stores:
-        store.wait()
+
+
+def deal(merged, gain, o_out, dq_out, dk_out, dv_out, gain_out, sem):
+    copies = [
+        pltpu.make_async_copy(merged.at[i], ref, sem.at[i])
+        for i, ref in enumerate((o_out, dq_out, dk_out, dv_out))
+    ]
+    for copy in copies:
+        copy.start()
+    gain_out[...] = gain[...]
+    for copy in copies:
+        copy.wait()
 
 
 def body(queries, keys, values, out_grad, gains, keep_order, keep_count):
@@ -388,12 +417,13 @@
     turned = pltpu.VMEM((HD, KEPT), BF)
     dma = pltpu.SemaphoreType.DMA
     out = jax.ShapeDtypeStruct((DEV, TS, HD), BF)
-    results = pl.pallas_call(
+    gain_shape = jax.ShapeDtypeStruct((2, HD), F32)
+    merged, gain = pl.pallas_call(
         kernel,
-        out_shape=[out] * 4 + [jax.ShapeDtypeStruct((2, HD), F32)],
+        out_shape=[pltpu.VMEM((4, DEV, TS, HD), BF), pltpu.VMEM((2, HD), F32)],
         in_specs=[vmem, vmem, vmem, smem] + [hbm] * 4,
-        out_specs=[hbm] * 4 + [vmem],
-        scratch_shapes=[pltpu.VMEM((4, DEV, TS, HD), BF)] * 2
+        out_specs=[vmem, vmem],
+        scratch_shapes=[pltpu.VMEM((4, DEV, TS, HD), BF)]
         + [message] * 8
         + [pltpu.VMEM((2, MSG, TS), BF)] * 2
         + [pltpu.VMEM((2, 2 * TS, MSG), BF)]
@@ -406,13 +436,22 @@
         + [result] * 4
         + [pltpu.VMEM((8, HD), F32), pltpu.VMEM((DEV, 8, HD), F32)]
         + [pltpu.VMEM((8, HD), F32), pltpu.VMEM((DP, 8, HD), F32)]
+        + [pltpu.VMEM((2, 8, HD), F32)]
         + [pltpu.SMEM((DEV,), jnp.int32)]
-        + [dma((4,)), dma((4,)), dma((3,)), dma((3,)), dma((2,)), dma((2,))]
-        + [dma, dma((DEV,)), dma((2,)), dma((2,))],
+        + [dma((4,)), dma((3,)), dma((3,)), dma((2,)), dma((2,))]
+        + [dma, dma((DEV,)), dma((3,)), dma((3,))],
         compiler_params=pltpu.CompilerParams(
             collective_id=0, has_side_effects=True, vmem_limit_bytes=60 * 1024 * 1024
         ),
     )(gains, keep_order, keep_count, keep_count, *pairs)
+    results = pl.pallas_call(
+        deal,
+        out_shape=[out] * 4 + [gain_shape],
+        in_specs=[vmem, vmem],
+        out_specs=[hbm] * 4 + [vmem],
+        scratch_shapes=[dma((4,))],
+        compiler_params=pltpu.CompilerParams(vmem_limit_bytes=8 * 1024 * 1024),
+    )(merged, gain)
     shape = queries.shape
     return tuple(r.reshape(shape) for r in results[:4]) + (results[4],)
 

time: 112 us -> 106 us (0.946); the launches traced: 110 us -> 106 us
  local copies, waits for them, and re-layouts: 5.92 us -> 0 us
    unnamed x13 -> x0, local copies, waits for them, and re-layouts: 5.92 us -> none
    pallas_call x1 -> x2, Pallas kernels: 104 us -> 105 us  [the longest x1 103 us: body(): pl.pallas_call(kernel, out_shape=[pltpu.VMEM((4, DEV, TS, HD), BF), pltpu...]
where the time goes in v2:
time: 106 us
  Pallas kernels  105 us (99%)
    pallas_call x1, Pallas kernels, body(): pl.pallas_call(kernel, out_shape=[pltpu.VMEM((4, DEV, TS, HD), BF), pltpu...  103 us

profile of v2, /device:TPU:1, one launch (start us, length us, event | category | flops | bytes accessed | tf_op | source)
XLA Modules:
  0.0 105.8 jit_solution(12642303121714543064)
XLA Ops:
  0.6 103.1 %shard_map.110 = (bf16[4,32,72,128]{3,2,1,0:T(8,128)(2,1)S(1)}, f32[2,128]{1,0:T(2,128)S(1)}) custom-call(f32[2,128]{1,0:T(2,128)} %gains.1, s32[2,32,72]{2,1,0:T(8,128)} %order.1, s32[2,32]{1,0:T(2,128)} %count_s.1, s32[2,32]{1,0:T(2,128)} %count_s.1, bf16[32,72,128]{2,1,0:T(8,128)(2,1)} %bitcast.8, bf16[32,72,128]{2,1,0:T(8,128)(2,1)} %bitcast.9, ...), custom_call_target="tpu_custom_call" | custom-call | tf_op jit(solution)/shard_map/pallas_call | solution.py:421
  103.8 2.0 %shard_map.111 = (bf16[32,72,128]{2,1,0:T(8,128)(2,1)}, bf16[32,72,128]{2,1,0:T(8,128)(2,1)}, bf16[32,72,128]{2,1,0:T(8,128)(2,1)}, bf16[32,72,128]{2,1,0:T(8,128)(2,1)}, f32[2,128]{1,0:T(2,128)}) custom-call(bf16[4,32,72,128]{3,2,1,0:T(8,128)(2,1)S(1)} %get-tuple-element.12.merged, f32[2,128]{1,0:T(2,128)S(1)} %get-tuple-element.13.gain), custom_call_target="tpu_custom_call" | custom-call | tf_op jit(solution)/shard_map/pallas_call | solution.py:447

commit v3 on v2

--- a/solution.py
+++ b/solution.py
@@ -52,7 +52,7 @@
     pack_a, pack_b, unpack, hot_a, hot_b, place_a, place_b,
     prob, prob_b, ds_b, qn, kn, vv, gg, uq, uk, iq, ik, qn_t, gg_t,
     y_o, y_dv, y_dq, y_dk, gsend, gbuf, hsend, hbuf, total, starts,
-    in_sem, fs, fr, bs, br, dds, ddr, gs, gr,
+    met, in_sem, fs, fr, bs, br, dds, ddr, gs, gr,
 ):
     me = lax.axis_index("ctx")
     dp = lax.axis_index("dp")
@@ -65,18 +65,28 @@
     def behind(k):
         return lax.rem(me + DEV - k, DEV)
 
-    def spread(step):
+    def pairs(lo, hi, step):
         def both(k):
             step(k)
             step(DEV - k)
 
-        loop(1, DEV // 2, both)
+        loop(lo, hi, both)
+
+    def spread(step):
+        pairs(1, DEV // 2, step)
         step(DEV // 2)
 
     is_hub = me == 0
     barrier = pltpu.get_barrier_semaphore()
-    loop(1, DEV, lambda k: pl.semaphore_signal(
-        barrier, inc=1, device_id={"ctx": ahead(k)}, device_id_type=MESH))
+
+    def greet(k):
+        @pl.when(ahead(k) != 0)
+        def _():
+            pl.semaphore_signal(
+                barrier, inc=1, device_id={"ctx": ahead(k)}, device_id_type=MESH
+            )
+
+    loop(1, DEV, greet)
 
     @pl.when(is_hub)
     def _():
@@ -116,20 +126,14 @@
         rows = (dot(pack_a[s], first) + dot(pack_b[s], second)).astype(BF)
         return rows[:, :HD], rows[:, HD:]
 
-    recv_qk[0], recv_vg[0] = packed(0)
-
-    def pack(k):
-        send_qk[k], send_vg[k] = packed(k)
-
-    loop(1, DEV, pack)
+    @pl.when(jnp.logical_not(is_hub))
+    def _():
+        pl.semaphore_wait(barrier, DEV - 1)
+        pl.semaphore_signal(met, inc=1, device_id={"ctx": 0}, device_id_type=MESH)
 
     @pl.when(is_hub)
     def _():
-        pl.semaphore_wait(barrier, DEV - 1 + DP - 1)
-
-    @pl.when(jnp.logical_not(is_hub))
-    def _():
-        pl.semaphore_wait(barrier, DEV - 1)
+        pl.semaphore_wait(met, DEV - 1)
 
     def remote(src, dst, send_sem, recv_sem, peer):
         return pltpu.make_async_remote_copy(
@@ -144,8 +148,11 @@
 
     every = pl.ds(1, DEV - 1)
 
-    spread(lambda k: part(
-        send_qk, recv_qk, k, 0, MSG, fs.at[0], fr.at[0], ahead(k)).start())
+    def pack(k):
+        send_qk[k], send_vg[k] = packed(k)
+        part(send_qk, recv_qk, k, 0, MSG, fs.at[0], fr.at[0], ahead(k)).start()
+
+    spread(pack)
     spread(lambda k: part(
         send_vg, recv_vg, k, 0, HALF, fs.at[1], fr.at[1], ahead(k)).start())
     spread(lambda k: part(
@@ -153,6 +160,8 @@
     all_qk = part(send_qk, recv_qk, every, 0, MSG, fs.at[0], fr.at[0], ahead(1))
     all_v = part(send_vg, recv_vg, every, 0, HALF, fs.at[1], fr.at[1], ahead(1))
     all_g = part(send_vg, recv_vg, every, HALF, MAIN, fs.at[2], fr.at[2], ahead(1))
+
+    recv_qk[0], recv_vg[0] = packed(0)
 
     def add_start(c, total):
         starts[c] = total
@@ -324,6 +333,20 @@
     def _():
         to_hub.start()
 
+    def grad_rows(k):
+        return main_rows(y_dq, k), tail_rows(y_dq, y_dk, k), main_rows(y_dk, k)
+
+    recv_dd[0, 0:MAIN], recv_dd[0, MAIN:HALF], recv_dd[0, HALF:MSG] = grad_rows(0)
+
+    def back_dd(k):
+        return part(send_dd, recv_dd, k, 0, MSG, dds, ddr.at[k], behind(k))
+
+    def grad_main(k):
+        send_dd[k, 0:MAIN], send_dd[k, MAIN:HALF], send_dd[k, HALF:MSG] = grad_rows(k)
+        back_dd(k).start()
+
+    spread(grad_main)
+
     @pl.when(is_hub)
     def _():
         gbuf[0] = gsend[...]
@@ -332,7 +355,23 @@
             0, DEV, lambda c, acc: acc + gbuf[c], jnp.zeros((8, HD), F32)
         )
         hbuf[0] = hsend[...]
+        pl.semaphore_wait(barrier, DP - 1)
         loop(1, DP, lambda k: between(hsend, hbuf.at[k], k).start())
+
+    all_dd = part(send_dd, recv_dd, every, 0, MSG, dds, ddr.at[0], behind(1))
+
+    all_o.wait_recv()
+    all_dv.wait_recv()
+
+    def home(k, recv, first, second):
+        pair = ahead(k)
+        rows = dot(unpack[pair // HEADS], recv[k]).astype(BF)
+        outs[first, pair] = rows[:TS]
+        outs[second, pair] = rows[TS:]
+
+    loop(0, DEV, lambda k: home(k, recv_ov, 0, 3))
+    @pl.when(is_hub)
+    def _():
         between(hbuf.at[others], hbuf.at[others], 1).wait_recv()
         total[0] = lax.fori_loop(
             0, DP, lambda c, acc: acc + hbuf[lax.rem(dp + DP - c, DP)], jnp.zeros((8, HD), F32)
@@ -340,31 +379,6 @@
         total[1] = total[0]
         loop(1, DEV, lambda k: to_group(k).start())
 
-    def grad_rows(k):
-        return main_rows(y_dq, k), tail_rows(y_dq, y_dk, k), main_rows(y_dk, k)
-
-    recv_dd[0, 0:MAIN], recv_dd[0, MAIN:HALF], recv_dd[0, HALF:MSG] = grad_rows(0)
-
-    def back_dd(k):
-        return part(send_dd, recv_dd, k, 0, MSG, dds, ddr.at[k], behind(k))
-
-    def grad_main(k):
-        send_dd[k, 0:MAIN], send_dd[k, MAIN:HALF], send_dd[k, HALF:MSG] = grad_rows(k)
-        back_dd(k).start()
-
-    spread(grad_main)
-    all_dd = part(send_dd, recv_dd, every, 0, MSG, dds, ddr.at[0], behind(1))
-
-    all_o.wait_recv()
-    all_dv.wait_recv()
-
-    def home(k, recv, first, second):
-        pair = ahead(k)
-        rows = dot(unpack[pair // HEADS], recv[k]).astype(BF)
-        outs[first, pair] = rows[:TS]
-        outs[second, pair] = rows[TS:]
-
-    loop(0, DEV, lambda k: home(k, recv_ov, 0, 3))
     home(0, recv_dd, 1, 2)
 
     def last(k):
@@ -393,7 +407,9 @@
 
 def deal(merged, gain, o_out, dq_out, dk_out, dv_out, gain_out, sem):
     copies = [
-        pltpu.make_async_copy(merged.at[i], ref, sem.at[i])
+        pltpu.make_async_copy(merged.at[i, rows], ref.at[rows], sem.at[i, n])
+        for n in range(4)
+        for rows in (pl.ds(n * (DEV // 4), DEV // 4),)
         for i, ref in enumerate((o_out, dq_out, dk_out, dv_out))
     ]
     for copy in copies:
@@ -438,7 +454,7 @@
         + [pltpu.VMEM((8, HD), F32), pltpu.VMEM((DP, 8, HD), F32)]
         + [pltpu.VMEM((2, 8, HD), F32)]
         + [pltpu.SMEM((DEV,), jnp.int32)]
-        + [dma((4,)), dma((3,)), dma((3,)), dma((2,)), dma((2,))]
+        + [pltpu.SemaphoreType.REGULAR, dma((4,)), dma((3,)), dma((3,)), dma((2,)), dma((2,))]
         + [dma, dma((DEV,)), dma((3,)), dma((3,))],
         compiler_params=pltpu.CompilerParams(
             collective_id=0, has_side_effects=True, vmem_limit_bytes=60 * 1024 * 1024
@@ -449,7 +465,7 @@
         out_shape=[out] * 4 + [gain_shape],
         in_specs=[vmem, vmem],
         out_specs=[hbm] * 4 + [vmem],
-        scratch_shapes=[dma((4,))],
+        scratch_shapes=[dma((4, 4))],
         compiler_params=pltpu.CompilerParams(vmem_limit_bytes=8 * 1024 * 1024),
     )(merged, gain)
     shape = queries.shape

time: 106 us -> 98.4 us (0.928)
  Pallas kernels: 105 us -> 97.5 us
    pallas_call x1, Pallas kernels: 103 us -> 95.4 us  [body(): pl.pallas_call(kernel, out_shape=[pltpu.VMEM((4, DEV, TS, HD), BF), pltpu...]
where the time goes in v3:
time: 98.4 us; the launch traced here: 98.2 us
  Pallas kernels  97.5 us (99%)
    pallas_call x1, Pallas kernels, body(): pl.pallas_call(kernel, out_shape=[pltpu.VMEM((4, DEV, TS, HD), BF), pltpu...  95.4 us
    pallas_call x1, Pallas kernels, body(): pl.pallas_call(deal, out_shape=[out] * 4 + [gain_shape], in_specs=[vmem,...  2.09 us

profile of v3, /device:TPU:1, one launch (start us, length us, event | category | flops | bytes accessed | tf_op | source)
XLA Modules:
  0.0 98.2 jit_solution(17996962984436091403)
XLA Ops:
  0.6 95.4 %shard_map.110 = (bf16[4,32,72,128]{3,2,1,0:T(8,128)(2,1)S(1)}, f32[2,128]{1,0:T(2,128)S(1)}) custom-call(f32[2,128]{1,0:T(2,128)} %gains.1, s32[2,32,72]{2,1,0:T(8,128)} %order.1, s32[2,32]{1,0:T(2,128)} %count_s.1, s32[2,32]{1,0:T(2,128)} %count_s.1, bf16[32,72,128]{2,1,0:T(8,128)(2,1)} %bitcast.8, bf16[32,72,128]{2,1,0:T(8,128)(2,1)} %bitcast.9, ...), custom_call_target="tpu_custom_call" | custom-call | tf_op jit(solution)/shard_map/pallas_call | solution.py:437
  96.1 2.1 %shard_map.111 = (bf16[32,72,128]{2,1,0:T(8,128)(2,1)}, bf16[32,72,128]{2,1,0:T(8,128)(2,1)}, bf16[32,72,128]{2,1,0:T(8,128)(2,1)}, bf16[32,72,128]{2,1,0:T(8,128)(2,1)}, f32[2,128]{1,0:T(2,128)}) custom-call(bf16[4,32,72,128]{3,2,1,0:T(8,128)(2,1)S(1)} %get-tuple-element.12.merged, f32[2,128]{1,0:T(2,128)S(1)} %get-tuple-element.13.gain), custom_call_target="tpu_custom_call" | custom-call | tf_op jit(solution)/shard_map/pallas_call | solution.py:463

commit v4 on v3

--- a/solution.py
+++ b/solution.py
@@ -11,6 +11,7 @@
 F32 = jnp.float32
 
 DEV = 32
+NY, NX = 8, 4
 DP = 16
 HEADS = 16
 TS = 72
@@ -52,7 +53,7 @@
     pack_a, pack_b, unpack, hot_a, hot_b, place_a, place_b,
     prob, prob_b, ds_b, qn, kn, vv, gg, uq, uk, iq, ik, qn_t, gg_t,
     y_o, y_dv, y_dq, y_dk, gsend, gbuf, hsend, hbuf, total, starts,
-    met, in_sem, fs, fr, bs, br, dds, ddr, gs, gr,
+    met, rowed, in_sem, fs, fr, bs, br, dds, ddr, gs, gr,
 ):
     me = lax.axis_index("ctx")
     dp = lax.axis_index("dp")
@@ -76,17 +77,26 @@
         pairs(1, DEV // 2, step)
         step(DEV // 2)
 
+    y, x = me // NX, lax.rem(me, NX)
+
+    def partner(j, i):
+        return lax.rem(y + j, NY) * NX + lax.rem(x + i, NX)
+
+    def step_to(j, i):
+        return lax.rem(partner(j, i) - me + DEV, DEV)
+
     is_hub = me == 0
     barrier = pltpu.get_barrier_semaphore()
 
-    def greet(k):
-        @pl.when(ahead(k) != 0)
+    def greet(device):
+        @pl.when(device != 0)
         def _():
             pl.semaphore_signal(
-                barrier, inc=1, device_id={"ctx": ahead(k)}, device_id_type=MESH
+                barrier, inc=1, device_id={"ctx": device}, device_id_type=MESH
             )
 
-    loop(1, DEV, greet)
+    loop(1, NY, lambda j: greet(partner(j, 0)))
+    loop(1, NX, lambda i: greet(partner(0, i)))
 
     @pl.when(is_hub)
     def _():
@@ -128,12 +138,18 @@
 
     @pl.when(jnp.logical_not(is_hub))
     def _():
-        pl.semaphore_wait(barrier, DEV - 1)
-        pl.semaphore_signal(met, inc=1, device_id={"ctx": 0}, device_id_type=MESH)
+        pl.semaphore_wait(barrier, NY - 1 + NX - 1)
+
+        @pl.when(x * y == 0)
+        def _():
+            pl.semaphore_signal(met, inc=1, device_id={"ctx": 0}, device_id_type=MESH)
 
     @pl.when(is_hub)
     def _():
-        pl.semaphore_wait(met, DEV - 1)
+        pl.semaphore_wait(met, NY - 1 + NX - 1)
+
+    loop(1, NY, lambda j: pl.semaphore_signal(
+        rowed, inc=1, device_id={"ctx": partner(j, 0)}, device_id_type=MESH))
 
     def remote(src, dst, send_sem, recv_sem, peer):
         return pltpu.make_async_remote_copy(
@@ -148,11 +164,24 @@
 
     every = pl.ds(1, DEV - 1)
 
-    def pack(k):
-        send_qk[k], send_vg[k] = packed(k)
-        part(send_qk, recv_qk, k, 0, MSG, fs.at[0], fr.at[0], ahead(k)).start()
-
-    spread(pack)
+    def pack(*steps):
+        rows = [packed(k) for k in steps]
+        for k, (first, second) in zip(steps, rows, strict=True):
+            send_qk[k], send_vg[k] = first, second
+        for k in steps:
+            part(send_qk, recv_qk, k, 0, MSG, fs.at[0], fr.at[0], ahead(k)).start()
+
+    loop(1, NY // 2, lambda j: pack(step_to(j, 0), step_to(NY - j, 0)))
+    pack(step_to(0, 1), step_to(0, 3))
+    pack(step_to(NY // 2, 0), step_to(0, 2))
+    pl.semaphore_wait(rowed, NY - 1)
+
+    def pack_others(n):
+        j, i = 1 + n // (NX - 1), 1 + lax.rem(n, NX - 1)
+        pack(step_to(j, i), step_to(NY - j, i))
+
+    loop(0, (NY // 2 - 1) * (NX - 1), pack_others)
+    loop(1, NX, lambda i: pack(step_to(NY // 2, i)))
     spread(lambda k: part(
         send_vg, recv_vg, k, 0, HALF, fs.at[1], fr.at[1], ahead(k)).start())
     spread(lambda k: part(
@@ -454,7 +483,8 @@
         + [pltpu.VMEM((8, HD), F32), pltpu.VMEM((DP, 8, HD), F32)]
         + [pltpu.VMEM((2, 8, HD), F32)]
         + [pltpu.SMEM((DEV,), jnp.int32)]
-        + [pltpu.SemaphoreType.REGULAR, dma((4,)), dma((3,)), dma((3,)), dma((2,)), dma((2,))]
+        + [pltpu.SemaphoreType.REGULAR] * 2
+        + [dma((4,)), dma((3,)), dma((3,)), dma((2,)), dma((2,))]
         + [dma, dma((DEV,)), dma((3,)), dma((3,))],
         compiler_params=pltpu.CompilerParams(
             collective_id=0, has_side_effects=True, vmem_limit_bytes=60 * 1024 * 1024

time: 98.4 us -> 95.4 us (0.970)
  Pallas kernels: 97.5 us -> 93.8 us
    pallas_call x1, Pallas kernels: 95.4 us -> 91.7 us  [body(): pl.pallas_call(kernel, out_shape=[pltpu.VMEM((4, DEV, TS, HD), BF), pltpu...]
where the time goes in v4:
time: 95.4 us; the launch traced here: 94.5 us
  Pallas kernels  93.8 us (98%)
    pallas_call x1, Pallas kernels, body(): pl.pallas_call(kernel, out_shape=[pltpu.VMEM((4, DEV, TS, HD), BF), pltpu...  91.7 us
    pallas_call x1, Pallas kernels, body(): pl.pallas_call(deal, out_shape=[out] * 4 + [gain_shape], in_specs=[vmem,...  2.09 us

profile of v4, /device:TPU:1, one launch (start us, length us, event | category | flops | bytes accessed | tf_op | source)
XLA Modules:
  0.0 94.5 jit_solution(4494244496534401780)
XLA Ops:
  0.6 91.7 %shard_map.110 = (bf16[4,32,72,128]{3,2,1,0:T(8,128)(2,1)S(1)}, f32[2,128]{1,0:T(2,128)S(1)}) custom-call(f32[2,128]{1,0:T(2,128)} %gains.1, s32[2,32,72]{2,1,0:T(8,128)} %order.1, s32[2,32]{1,0:T(2,128)} %count_s.1, s32[2,32]{1,0:T(2,128)} %count_s.1, bf16[32,72,128]{2,1,0:T(8,128)(2,1)} %bitcast.8, bf16[32,72,128]{2,1,0:T(8,128)(2,1)} %bitcast.9, ...), custom_call_target="tpu_custom_call" | custom-call | tf_op jit(solution)/shard_map/pallas_call | solution.py:466
  92.4 2.1 %shard_map.111 = (bf16[32,72,128]{2,1,0:T(8,128)(2,1)}, bf16[32,72,128]{2,1,0:T(8,128)(2,1)}, bf16[32,72,128]{2,1,0:T(8,128)(2,1)}, bf16[32,72,128]{2,1,0:T(8,128)(2,1)}, f32[2,128]{1,0:T(2,128)}) custom-call(bf16[4,32,72,128]{3,2,1,0:T(8,128)(2,1)S(1)} %get-tuple-element.12.merged, f32[2,128]{1,0:T(2,128)S(1)} %get-tuple-element.13.gain), custom_call_target="tpu_custom_call" | custom-call | tf_op jit(solution)/shard_map/pallas_call | solution.py:493

commit v5 on v4

--- a/solution.py
+++ b/solution.py
@@ -47,9 +47,9 @@
 
 
 def kernel(
-    gains, order, count_v, count_s, q_hbm, k_hbm, v_hbm, g_hbm,
+    gains_hbm, order_hbm, count_hbm, q_hbm, k_hbm, v_hbm, g_hbm,
     outs, gain_out,
-    xs, send_qk, send_vg, recv_qk, recv_vg, send_ov, send_dd, recv_ov, recv_dd,
+    gains, order, count_v, count_s, xs, send_qk, send_vg, recv_qk, recv_vg, send_ov, send_dd, recv_ov, recv_dd,
     pack_a, pack_b, unpack, hot_a, hot_b, place_a, place_b,
     prob, prob_b, ds_b, qn, kn, vv, gg, uq, uk, iq, ik, qn_t, gg_t,
     y_o, y_dv, y_dq, y_dk, gsend, gbuf, hsend, hbuf, total, starts,
@@ -103,12 +103,20 @@
         loop(1, DP, lambda k: pl.semaphore_signal(
             barrier, inc=1, device_id={"dp": lax.rem(dp + k, DP)}, device_id_type=MESH))
 
+    small = [
+        pltpu.make_async_copy(ref, into, in_sem.at[4 + i])
+        for i, (ref, into) in enumerate(
+            ((order_hbm, order), (count_hbm, count_s), (count_hbm, count_v), (gains_hbm, gains))
+        )
+    ]
     loads = [
         pltpu.make_async_copy(ref, xs.at[i], in_sem.at[i])
         for i, ref in enumerate((q_hbm, k_hbm, v_hbm, g_hbm))
     ]
-    for load in loads:
+    for load in small + loads:
         load.start()
+    for load in small:
+        load.wait()
 
     row, slot = iota((MSG, TS), 0), iota((MSG, TS), 1)
     pick_a = ((row == slot) & (row < 54)).astype(F32).astype(BF)
@@ -451,7 +459,6 @@
 def body(queries, keys, values, out_grad, gains, keep_order, keep_count):
     pairs = [x.reshape(DEV, TS, HD) for x in (queries, keys, values, out_grad)]
     vmem = pl.BlockSpec(memory_space=pltpu.VMEM)
-    smem = pl.BlockSpec(memory_space=pltpu.SMEM)
     hbm = pl.BlockSpec(memory_space=pl.ANY)
     message = pltpu.VMEM((DEV, MSG, HD), BF)
     rows_b, rows_f = pltpu.VMEM((KEPT, HD), BF), pltpu.VMEM((KEPT, HD), F32)
@@ -466,9 +473,11 @@
     merged, gain = pl.pallas_call(
         kernel,
         out_shape=[pltpu.VMEM((4, DEV, TS, HD), BF), pltpu.VMEM((2, HD), F32)],
-        in_specs=[vmem, vmem, vmem, smem] + [hbm] * 4,
+        in_specs=[hbm] * 7,
         out_specs=[vmem, vmem],
-        scratch_shapes=[pltpu.VMEM((4, DEV, TS, HD), BF)]
+        scratch_shapes=[pltpu.VMEM((2, HD), F32), pltpu.VMEM((2, DEV, TS), jnp.int32)]
+        + [pltpu.VMEM((2, DEV), jnp.int32), pltpu.SMEM((2, DEV), jnp.int32)]
+        + [pltpu.VMEM((4, DEV, TS, HD), BF)]
         + [message] * 8
         + [pltpu.VMEM((2, MSG, TS), BF)] * 2
         + [pltpu.VMEM((2, 2 * TS, MSG), BF)]
@@ -484,12 +493,12 @@
         + [pltpu.VMEM((2, 8, HD), F32)]
         + [pltpu.SMEM((DEV,), jnp.int32)]
         + [pltpu.SemaphoreType.REGULAR] * 2
-        + [dma((4,)), dma((3,)), dma((3,)), dma((2,)), dma((2,))]
+        + [dma((8,)), dma((3,)), dma((3,)), dma((2,)), dma((2,))]
         + [dma, dma((DEV,)), dma((3,)), dma((3,))],
         compiler_params=pltpu.CompilerParams(
             collective_id=0, has_side_effects=True, vmem_limit_bytes=60 * 1024 * 1024
         ),
-    )(gains, keep_order, keep_count, keep_count, *pairs)
+    )(gains, keep_order, keep_count, *pairs)
     results = pl.pallas_call(
         deal,
         out_shape=[out] * 4 + [gain_shape],

time: 95.4 us -> 94.5 us (level)
  no operation moved by 1% of the time
where the time goes in v5:
time: 94.5 us; the launch traced here: 93.7 us
  Pallas kernels  93.1 us (99%)
    pallas_call x1, Pallas kernels, body(): pl.pallas_call(kernel, out_shape=[pltpu.VMEM((4, DEV, TS, HD), BF), pltpu...  91 us
    pallas_call x1, Pallas kernels, body(): pl.pallas_call(deal, out_shape=[out] * 4 + [gain_shape], in_specs=[vmem,...  2.09 us

profile of v5, /device:TPU:1, one launch (start us, length us, event | category | flops | bytes accessed | tf_op | source)
XLA Modules:
  0.0 93.7 jit_solution(14743199852373870560)
XLA Ops:
  0.6 91.0 %shard_map.110 = (bf16[4,32,72,128]{3,2,1,0:T(8,128)(2,1)S(1)}, f32[2,128]{1,0:T(2,128)S(1)}) custom-call(f32[2,128]{1,0:T(2,128)} %gains_hbm.1, s32[2,32,72]{2,1,0:T(8,128)} %order_hbm.1, s32[2,32]{1,0:T(2,128)} %count_hbm.1, bf16[32,72,128]{2,1,0:T(8,128)(2,1)} %bitcast.8, bf16[32,72,128]{2,1,0:T(8,128)(2,1)} %bitcast.9, bf16[32,72,128]{2,1,0:T(8,128)(2,1)} %bitcast.10, ...), custom_call_target="tpu_custom_call" | custom-call | tf_op jit(solution)/shard_map/pallas_call | solution.py:473
  91.6 2.1 %shard_map.111 = (bf16[32,72,128]{2,1,0:T(8,128)(2,1)}, bf16[32,72,128]{2,1,0:T(8,128)(2,1)}, bf16[32,72,128]{2,1,0:T(8,128)(2,1)}, bf16[32,72,128]{2,1,0:T(8,128)(2,1)}, f32[2,128]{1,0:T(2,128)}) custom-call(bf16[4,32,72,128]{3,2,1,0:T(8,128)(2,1)S(1)} %get-tuple-element.12.merged, f32[2,128]{1,0:T(2,128)S(1)} %get-tuple-element.13.gain), custom_call_target="tpu_custom_call" | custom-call | tf_op jit(solution)/shard_map/pallas_call | solution.py:502
